TPU v7x, 128 devices: a whole 4x4x4 slice. The times are simulated.
128 devices in a mesh: row: 8 (over x, core), col: 16 (over z, y).
Axes of the slice: x: 4, y: 4, z: 4, core: 2. Of those that a mesh axis runs over, the one named last changes fastest.
Arguments:
- density: bfloat16 [6144, 6144], P('row', 'col'), may hold values from -5 to 5
- strips: bfloat16 [16384, 8, 128], P(('row', 'col')), may hold values from -5 to 5
- dest_device: int32 [16384, 1], P(('row', 'col')), may hold values from 0 to 127; in each aligned block of 128 rows (0 to 127, 128 to 255, ...) at most 2 rows name the same one
- atom_slot: int32 [16384], P(('row', 'col')), may hold values from 0 to 95
- block_slot: int32 [16384], P(('row', 'col')), may hold values from 0 to 2
- patterns: int32 [3, 48, 48], replicated, may hold values 0 or 1
Outputs:
- density_next: float32 [6144, 6144], P('row', 'col')
- response_next: float32 [6144, 6144], P('row', 'col')
Inputs may be any that keep to these rules, and one draw needn't show every extreme that they name: `dest_device`: of the 128 strips of one device, at most 2 name the same owner, and some owner is named that often.
All inputs are finite; a program needn't handle non-finite values.
Results may differ from a plain program's by a relative error of at most 0.0036.
Values may be sent and summed in bfloat16 or wider, within the bound.
A program may use at most 128 MiB of HBM per device.

v0:
```python
import math
import jax
import jax.numpy as jnp
from jax import lax
from jax.sharding import PartitionSpec as P

STEPS = 2
CAPACITY = 2


def tile_kept(patterns, which, row_offset, col_offset, block_rows, block_cols, block_width):
    window = lax.dynamic_slice(patterns[which], (row_offset, col_offset), (block_rows, block_cols))
    global_rows = row_offset + lax.iota(jnp.int32, block_rows)
    global_cols = col_offset + lax.iota(jnp.int32, block_cols)
    diagonal = (global_rows[:, None] == global_cols[None, :]).astype(jnp.int32)
    kept = jnp.maximum(window, diagonal).astype(jnp.float32)
    return jnp.repeat(jnp.repeat(kept, block_width, axis=0), block_width, axis=1)


def products(zeroth, linear):
    col_zero, col_first = (
        lax.all_gather(zeroth, "row", axis=0, tiled=True),
        lax.all_gather(linear, "row", axis=0, tiled=True),
    )
    pieces = (
        lax.all_gather(zeroth, "col", axis=1, tiled=True),
        lax.all_gather(linear, "col", axis=1, tiled=True),
    )
    square = jnp.dot(pieces[0], col_zero, preferred_element_type=jnp.float32)
    left_part = jnp.dot(pieces[0], col_first, preferred_element_type=jnp.float32)
    right_part = jnp.dot(pieces[1], col_zero, preferred_element_type=jnp.float32)
    return (square, left_part + right_part)


def on_device(density, strips, dest_device, atom_slot, block_slot, patterns):
    tile_rows, tile_cols = density.shape
    mesh_rows = lax.axis_size("row")
    mesh_cols = lax.axis_size("col")
    devices = mesh_rows * mesh_cols
    matrix_order = tile_rows * mesh_rows
    atom_width = strips.shape[1]
    block_width = strips.shape[2]
    block_rows = tile_rows // block_width
    block_cols = tile_cols // block_width
    row_offset = lax.axis_index("row") * block_rows
    col_offset = lax.axis_index("col") * block_cols
    kept_zero = tile_kept(patterns, 0, row_offset, col_offset, block_rows, block_cols, block_width)
    kept_first = tile_kept(patterns, 1, row_offset, col_offset, block_rows, block_cols, block_width)
    kept_field = tile_kept(patterns, 2, row_offset, col_offset, block_rows, block_cols, block_width)
    capacity = CAPACITY
    targets = dest_device[:, 0]
    order = lax.iota(jnp.int32, targets.shape[0])
    earlier = (targets[:, None] == targets[None, :]) & (order[None, :] < order[:, None])
    ranking = jnp.sum(earlier.astype(jnp.int32), axis=1)
    position = targets * capacity + ranking
    sent_strips = (
        jnp.zeros((devices * capacity, atom_width, block_width), strips.dtype)
        .at[position]
        .set(strips)
    )
    sent_atoms = jnp.full((devices * capacity,), -1, jnp.int32).at[position].set(atom_slot)
    sent_blocks = jnp.zeros((devices * capacity,), jnp.int32).at[position].set(block_slot)
    arrived = (
        lax.all_to_all(
            sent_strips.reshape(devices, capacity, atom_width, block_width),
            ("row", "col"),
            split_axis=0,
            concat_axis=0,
            tiled=True,
        ),
        lax.all_to_all(
            sent_atoms.reshape(devices, capacity),
            ("row", "col"),
            split_axis=0,
            concat_axis=0,
            tiled=True,
        ),
        lax.all_to_all(
            sent_blocks.reshape(devices, capacity),
            ("row", "col"),
            split_axis=0,
            concat_axis=0,
            tiled=True,
        ),
    )
    recv_strips = arrived[0].reshape(-1, atom_width * block_width)
    recv_atoms = arrived[1].reshape(-1)
    recv_blocks = arrived[2].reshape(-1)
    atoms_here = tile_rows // atom_width
    atom_match = recv_atoms[:, None] == lax.iota(jnp.int32, atoms_here)[None, :]
    block_match = recv_blocks[:, None] == lax.iota(jnp.int32, block_cols)[None, :]
    placing = (
        (atom_match[:, :, None] & block_match[:, None, :])
        .astype(jnp.bfloat16)
        .reshape(-1, atoms_here * block_cols)
    )
    summed = lax.dot_general(
        placing, recv_strips, (((0,), (0,)), ((), ())), preferred_element_type=jnp.float32
    )
    h_field = (
        summed.reshape(atoms_here, block_cols, atom_width, block_width)
        .transpose(0, 2, 1, 3)
        .reshape(tile_rows, tile_cols)
    )
    linear = (-(kept_field * h_field)).astype(jnp.bfloat16)
    zeroth = density
    inv_root = 1.0 / math.sqrt(matrix_order)
    new_zeroth = None
    new_linear = None
    for iteration in range(STEPS):
        square, crossed = products(zeroth, linear)
        if iteration % 2 == 0:
            new_zeroth = kept_zero * (square * inv_root)
            new_linear = kept_first * (crossed * inv_root)
        else:
            new_zeroth = kept_zero * (2.0 * zeroth.astype(jnp.float32) - square * inv_root)
            new_linear = kept_first * (2.0 * linear.astype(jnp.float32) - crossed * inv_root)
        zeroth = new_zeroth.astype(jnp.bfloat16)
        linear = new_linear.astype(jnp.bfloat16)
    return (new_zeroth, new_linear)


def solution(mesh):
    return jax.shard_map(
        on_device,
        mesh=mesh,
        in_specs=(
            P("row", "col"),
            P(("row", "col"), None, None),
            P(("row", "col"), None),
            P(("row", "col")),
            P(("row", "col")),
            P(),
        ),
        out_specs=(P("row", "col"), P("row", "col")),
        check_vma=False,
    )
```

profile of v0, /device:TPU:0, one launch (start us, length us, event | category | flops | bytes accessed | tf_op | source)
XLA Modules:
  0.0 540.9 jit_solution(16579620292933018582)
XLA Ops:
  7.9 0.9 convert_reduce_fusion
  9.5 1.1 scatter_custom_fusion.1
  10.6 0.8 all_to_all.17
  11.4 11.1 %all-to-all-start.1 = ((s32[128,1,2]{2,1,0:T(1,128)}), s32[128,1,2]{2,1,0:T(1,128)S(1)}, u32[]{:S(2)}, u32[]{:S(2)}) async-start(s32[128,1,2]{2,1,0:T(1,128)} %bitcast.10), calls=%async_computation.1 | async-start | bytes 131072 | tf_op jit(solution)/shard_map/all_to_all | solution.py:78
  22.5 0.8 fusion.23
  23.9 1.1 scatter_custom_fusion
  25.0 0.8 all_to_all.15
  25.8 6.5 %all-to-all-done.1 = s32[128,1,2]{2,1,0:T(1,128)S(1)} async-done(((s32[128,1,2]{2,1,0:T(1,128)}), s32[128,1,2]{2,1,0:T(1,128)S(1)}, u32[]{:S(2)}, u32[]{:S(2)}) %all-to-all-start.1) | async-done | bytes 1056 | tf_op jit(solution)/shard_map/all_to_all | solution.py:78
  32.2 4.6 all-to-all-start
  36.9 0.9 broadcast_in_dim.50
  37.8 13.4 %scatter_fusion = bf16[256,8,128]{2,1,0:T(8,128)(2,1)} fusion(bf16[256,8,128]{2,1,0:T(8,128)(2,1)} %broadcast_in_dim.50, s32[128]{0:T(128)S(1)} %fusion.18, bf16[128,8,128]{2,1,0:T(8,128)(2,1)S(1)} %copy-done.2), kind=kCustom, calls=%fused_computation.2 | custom fusion | bytes 786944 | tf_op jit(solution)/shard_map/scatter | solution.py:59
  51.7 0.8 reduce.6
  52.6 9.7 %all-to-all-start.2 = ((bf16[128,2,8,128]{3,2,1,0:T(8,128)(2,1)}), bf16[128,2,8,128]{3,2,1,0:T(8,128)(2,1)S(1)}, u32[]{:S(2)}, u32[]{:S(2)}) async-start(bf16[128,2,8,128]{3,2,1,0:T(8,128)(2,1)} %bitcast.13), calls=%async_computation.2 | async-start | bytes 1048576 | tf_op jit(solution)/shard_map/all_to_all | solution.py:64
  62.4 0.8 reduce.7
  63.7 12.2 %all-to-all-done.2 = bf16[128,2,8,128]{3,2,1,0:T(8,128)(2,1)S(1)} async-done(((bf16[128,2,8,128]{3,2,1,0:T(8,128)(2,1)}), bf16[128,2,8,128]{3,2,1,0:T(8,128)(2,1)S(1)}, u32[]{:S(2)}, u32[]{:S(2)}) %all-to-all-start.2) | async-done | bytes 524320 | tf_op jit(solution)/shard_map/all_to_all | solution.py:64
  76.6 0.7 copy.70
  77.7 0.9 fusion.12
  80.5 69.7 %all-gather.19.cloned.1.call-done = bf16[768,6144]{0,1:T(8,128)(2,1)} async-done(((bf16[768,384]{0,1:T(8,128)(2,1)}), bf16[768,6144]{0,1:T(8,128)(2,1)}) %all-gather.19.cloned.1.call-update) | async-done | bytes 9437200 | tf_op jit(solution)/shard_map/all_gather | solution.py:27
  150.2 9.0 %fusion.24 = f32[768,384]{1,0:T(8,128)S(1)} fusion(bf16[768,6144]{0,1:T(8,128)(2,1)} %all-gather.19.cloned.1.call-done, bf16[6144,384]{1,0:T(8,128)(2,1)} %all-gather.11.cloned.1.call-done), kind=kOutput, calls=%fused_computation.56 | convolution fusion | flops 3623878656 | bytes 15335424 | tf_op jit(solution)/shard_map/dot_general | solution.py:31
  159.3 27.1 %all-gather.17.cloned.1.call-done = bf16[6144,384]{0,1:T(8,128)(2,1)} async-done(((bf16[768,384]{0,1:T(8,128)(2,1)}), bf16[6144,384]{0,1:T(8,128)(2,1)}) %all-gather.17.cloned.1.call-update) | async-done | bytes 4718608 | tf_op jit(solution)/shard_map/all_gather | solution.py:23
  186.4 85.9 %all-gather.9.cloned.1.call-done = bf16[768,6144]{1,0:T(8,128)(2,1)} async-done(((bf16[768,384]{1,0:T(8,128)(2,1)}), bf16[768,6144]{1,0:T(8,128)(2,1)}) %all-gather.9.cloned.1.call-update) | async-done | bytes 9437200 | tf_op jit(solution)/shard_map/all_gather | solution.py:26
  272.2 9.8 %fusion.9 = bf16[768,384]{1,0:T(8,128)(2,1)} fusion(f32[768,384]{1,0:T(8,128)S(1)} %copy.54, f32[768,384]{1,0:T(8,128)S(1)} %fusion.24, bf16[6144,384]{0,1:T(8,128)(2,1)} %all-gather.17.cloned.1.call-done, bf16[768,6144]{1,0:T(8,128)(2,1)} %all-gather.9.cloned.1.call-done), kind=kOutput, calls=%fused_computation.17 | convolution fusion | flops 3625058304 | bytes 17104896 | tf_op jit(solution)/shard_map/dot_general | solution.py:30
  282.8 9.7 %fusion.10 = bf16[768,384]{1,0:T(8,128)(2,1)} fusion(f32[768,384]{1,0:T(8,128)S(1)} %copy.43, bf16[768,6144]{1,0:T(8,128)(2,1)} %all-gather.9.cloned.1.call-done, bf16[6144,384]{1,0:T(8,128)(2,1)} %all-gather.11.cloned.1.call-done), kind=kOutput, calls=%fused_computation.18 | convolution fusion | flops 3624763392 | bytes 15925248 | tf_op jit(solution)/shard_map/dot_general | solution.py:29
  292.6 0.7 all-gather.15.cloned.1.call-update
  293.4 0.7 all-gather.23.cloned.1.call-update
  294.1 21.6 %all-gather.21.cloned.1.call-done = bf16[6144,384]{1,0:T(8,128)(2,1)} async-done(((bf16[768,384]{1,0:T(8,128)(2,1)}), bf16[6144,384]{1,0:T(8,128)(2,1)}) %all-gather.21.cloned.1.call-update) | async-done | bytes 4718608 | tf_op jit(solution)/shard_map/all_gather | solution.py:23
  315.7 86.4 %all-gather.13.cloned.1.call-done = bf16[768,6144]{1,0:T(8,128)(2,1)} async-done(((bf16[768,384]{1,0:T(8,128)(2,1)}), bf16[768,6144]{1,0:T(8,128)(2,1)}) %all-gather.13.cloned.1.call-update) | async-done | bytes 9437200 | tf_op jit(solution)/shard_map/all_gather | solution.py:26
  402.2 9.8 %fusion.25 = f32[768,384]{1,0:T(8,128)} fusion(bf16[768,6144]{1,0:T(8,128)(2,1)} %all-gather.13.cloned.1.call-done, bf16[6144,384]{1,0:T(8,128)(2,1)} %all-gather.21.cloned.1.call-done), kind=kOutput, calls=%fused_computation.57 | convolution fusion | flops 3623878656 | bytes 15335424 | tf_op jit(solution)/shard_map/dot_general | solution.py:30
  411.9 26.0 %all-gather.15.cloned.1.call-done = bf16[6144,384]{1,0:T(8,128)(2,1)} async-done(((bf16[768,384]{1,0:T(8,128)(2,1)}), bf16[6144,384]{1,0:T(8,128)(2,1)}) %all-gather.15.cloned.1.call-update) | async-done | bytes 4718608 | tf_op jit(solution)/shard_map/all_gather | solution.py:22
  438.0 9.8 %fusion.2 = f32[768,384]{1,0:T(8,128)} fusion(f32[768,384]{1,0:T(8,128)S(1)} %copy.43, bf16[768,6144]{1,0:T(8,128)(2,1)} %all-gather.13.cloned.1.call-done, bf16[6144,384]{1,0:T(8,128)(2,1)} %all-gather.15.cloned.1.call-done, bf16[768,384]{1,0:T(8,128)(2,1)S(1)} %copy-done.1), kind=kOutput, calls=%fused_computation.9 | convolution fusion | flops 3625353216 | bytes 17104896 | tf_op jit(solution)/shard_map/dot_general | solution.py:29
  447.8 76.2 %all-gather.23.cloned.1.call-done = bf16[768,6144]{1,0:T(8,128)(2,1)} async-done(((bf16[768,384]{1,0:T(8,128)(2,1)}), bf16[768,6144]{1,0:T(8,128)(2,1)}) %all-gather.23.cloned.1.call-update) | async-done | bytes 9437200 | tf_op jit(solution)/shard_map/all_gather | solution.py:27
  524.0 10.1 %fusion.8 = f32[768,384]{1,0:T(8,128)} fusion(f32[768,384]{1,0:T(8,128)S(1)} %copy.54, f32[768,384]{1,0:T(8,128)} %fusion.25, bf16[768,6144]{1,0:T(8,128)(2,1)} %all-gather.23.cloned.1.call-done, bf16[6144,384]{1,0:T(8,128)(2,1)} %all-gather.15.cloned.1.call-done, bf16[768,384]{1,0:T(8,128)(2,1)S(1)} %copy-done), kind=kOutput, calls=%fused_computation.16 | convolution fusion | flops 3625648128 | bytes 18284544 | tf_op jit(solution)/shard_map/dot_general | solution.py:31
  (53 shorter events, 7.0 us)
Async XLA Ops:
  7.2 30.6 %copy-start.2 = (bf16[128,8,128]{2,1,0:T(8,128)(2,1)S(1)}, bf16[128,8,128]{2,1,0:T(8,128)(2,1)}, u32[]{:S(2)}) copy-start(bf16[128,8,128]{2,1,0:T(8,128)(2,1)} %param.7) | copy-start | bytes 786436
  7.2 73.4 %all-gather.11.cloned.1.call-start = ((), (), s32[]{:S(2)}) async-start(), calls=%async_computation.4 | async-start | bytes 5308416 | tf_op jit(solution)/shard_map/all_gather | solution.py:22
  11.4 20.8 %all-to-all-start.1 = ((s32[128,1,2]{2,1,0:T(1,128)}), s32[128,1,2]{2,1,0:T(1,128)S(1)}, u32[]{:S(2)}, u32[]{:S(2)}) async-start(s32[128,1,2]{2,1,0:T(1,128)} %bitcast.10), calls=%async_computation.1 | async-start | bytes 131072 | tf_op jit(solution)/shard_map/all_to_all | solution.py:78
  32.2 20.4 %all-to-all-start = ((s32[128,1,2]{2,1,0:T(1,128)}), s32[128,1,2]{2,1,0:T(1,128)S(1)}, u32[]{:S(2)}, u32[]{:S(2)}) async-start(s32[128,1,2]{2,1,0:T(1,128)} %bitcast.9), calls=%async_computation | async-start | bytes 131072 | tf_op jit(solution)/shard_map/all_to_all | solution.py:71
  52.6 23.3 %all-to-all-start.2 = ((bf16[128,2,8,128]{3,2,1,0:T(8,128)(2,1)}), bf16[128,2,8,128]{3,2,1,0:T(8,128)(2,1)S(1)}, u32[]{:S(2)}, u32[]{:S(2)}) async-start(bf16[128,2,8,128]{3,2,1,0:T(8,128)(2,1)} %bitcast.13), calls=%async_computation.2 | async-start | bytes 1048576 | tf_op jit(solution)/shard_map/all_to_all | solution.py:64
  62.3 87.9 %all-gather.19.cloned.1.call-start = ((), (), s32[]{:S(2)}) async-start(), calls=%async_computation.8 | async-start | bytes 10027008 | tf_op jit(solution)/shard_map/all_gather | solution.py:27
  78.6 107.8 %all-gather.17.cloned.1.call-start = ((), (), s32[]{:S(2)}) async-start(), calls=%async_computation.7 | async-start | bytes 5308416 | tf_op jit(solution)/shard_map/all_gather | solution.py:23
  79.3 192.9 %all-gather.9.cloned.1.call-start = ((), (), s32[]{:S(2)}) async-start(), calls=%async_computation.3 | async-start | bytes 10027008 | tf_op jit(solution)/shard_map/all_gather | solution.py:26
  79.9 235.8 %all-gather.21.cloned.1.call-start = ((), (), s32[]{:S(2)}) async-start(), calls=%async_computation.9 | async-start | bytes 5308416 | tf_op jit(solution)/shard_map/all_gather | solution.py:23
  282.1 120.1 %all-gather.13.cloned.1.call-start = ((), (), s32[]{:S(2)}) async-start(), calls=%async_computation.5 | async-start | bytes 10027008 | tf_op jit(solution)/shard_map/all_gather | solution.py:26
  292.6 145.4 %all-gather.15.cloned.1.call-start = ((), (), s32[]{:S(2)}) async-start(), calls=%async_computation.6 | async-start | bytes 5308416 | tf_op jit(solution)/shard_map/all_gather | solution.py:22
  293.3 230.6 %all-gather.23.cloned.1.call-start = ((), (), s32[]{:S(2)}) async-start(), calls=%async_computation.10 | async-start | bytes 10027008 | tf_op jit(solution)/shard_map/all_gather | solution.py:27
  294.1 143.9 %copy-start.1 = (bf16[768,384]{1,0:T(8,128)(2,1)S(1)}, bf16[768,384]{1,0:T(8,128)(2,1)}, u32[]{:S(2)}) copy-start(bf16[768,384]{1,0:T(8,128)(2,1)} %fusion.10) | copy-start | bytes 1769476
  411.9 112.0 %copy-start = (bf16[768,384]{1,0:T(8,128)(2,1)S(1)}, bf16[768,384]{1,0:T(8,128)(2,1)}, u32[]{:S(2)}) copy-start(bf16[768,384]{1,0:T(8,128)(2,1)} %fusion.9) | copy-start | bytes 1769476
Sparse Core Ops, SparseCore 0:
  9.7 37.7 all-gather.10
  78.7 71.4 all-gather.18
  152.5 33.8 all-gather.16
  188.4 83.8 all-gather.8
  282.2 33.4 all-gather.20
  318.3 83.8 all-gather.12
  404.4 33.4 all-gather.14
  440.1 83.8 all-gather.22
where the time goes:
time: 541 us
  waiting for transfers between devices  415 us (77%)
  matrix products  58.5 us (11%)
  starting transfers between devices  25.9 us (5%)
  local copies, waits for them, and re-layouts  22.8 us (4%)
  between operations  14.4 us (3%)
    all_gather x2, waiting for transfers between devices, products(): lax.all_gather(zeroth, 'col', axis=1, tiled=True)  172 us
    all_gather x2, waiting for transfers between devices, products(): lax.all_gather(linear, 'col', axis=1, tiled=True)  146 us
    all_gather x2, waiting for transfers between devices, products(): lax.all_gather(linear, 'row', axis=0, tiled=True)  48.8 us
    all_gather x2, waiting for transfers between devices, products(): lax.all_gather(zeroth, 'row', axis=0, tiled=True)  26 us
    dot_general x2, matrix products, products(): jnp.dot(pieces[0], col_first, preferred_element_type=jnp.float32)  19.6 us
    dot_general x2, matrix products, products(): square = jnp.dot(pieces[0], col_zero, preferred_element_type=jnp.float32)  19.5 us
    dot_general x2, matrix products, products(): jnp.dot(pieces[1], col_zero, preferred_element_type=jnp.float32)  19.1 us
    scatter x1, local copies, waits for them, and re-layouts, on_device(): sent_strips = jnp.zeros((devices * capacity, atom_width, block_width), st...  13.4 us
  transfers between devices with their start and end apart: 11, of which 9 were waited for; matrix products, arithmetic and copies ran while one was open for 12% of the time, Pallas kernels for 0%

commit v1 on v0

--- a/solution.py
+++ b/solution.py
@@ -3,6 +3,7 @@
 import jax.numpy as jnp
 from jax import lax
 from jax.sharding import PartitionSpec as P
+from jax.lax import all_to_all, axis_size
 
 STEPS = 2
 CAPACITY = 2
@@ -20,7 +21,7 @@
 def products(zeroth, linear):
     col_zero, col_first = (
         lax.all_gather(zeroth, "row", axis=0, tiled=True),
-        lax.all_gather(linear, "row", axis=0, tiled=True),
+        jnp.concatenate(all_to_all(jnp.stack(axis_size("row") * [linear], 0), "row", 0, 0), 0),
     )
     pieces = (
         lax.all_gather(zeroth, "col", axis=1, tiled=True),

time: 541 us -> 442 us (0.82)
  waiting for transfers between devices: 415 us -> 247 us
  blocking collectives: 0 us -> 60.2 us
    all_gather x2, waiting for transfers between devices: 172 us -> 65.4 us  [products(): lax.all_gather(zeroth, 'col', axis=1, tiled=True)]
    all_to_all x0 -> x1, blocking collectives: none -> 60.2 us  [products(): all_to_all(jnp.stack(axis_size('row') * [linear], 0), 'row', 0, 0)]
    all_gather x2 -> x0, waiting for transfers between devices: 48.8 us -> none  [products(): lax.all_gather(linear, 'row', axis=0, tiled=True)]
    all_gather x2, waiting for transfers between devices: 146 us -> 135 us  [products(): lax.all_gather(linear, 'col', axis=1, tiled=True)]
  transfers between devices with their start and end apart: 11 -> 10, of which waited for: 9 -> 7; matrix products, arithmetic and copies ran while one was open for 12% -> 17% of each run, Pallas kernels for 0% -> 0%
where the time goes in v1:
time: 442 us; the launch traced here: 441 us
  waiting for transfers between devices  247 us (56%)
  blocking collectives  60.2 us (14%)
  matrix products  59.2 us (13%)
  starting transfers between devices  30.5 us (7%)
  local copies, waits for them, and re-layouts  26.8 us (6%)
  between operations  14.4 us (3%)
    all_gather x2, waiting for transfers between devices, products(): lax.all_gather(linear, 'col', axis=1, tiled=True)  135 us
    all_gather x2, waiting for transfers between devices, products(): lax.all_gather(zeroth, 'col', axis=1, tiled=True)  65.4 us
    all_to_all x1, blocking collectives, products(): all_to_all(jnp.stack(axis_size('row') * [linear], 0), 'row', 0, 0)  60.2 us
    all_gather x2, waiting for transfers between devices, products(): lax.all_gather(zeroth, 'row', axis=0, tiled=True)  25.8 us
    dot_general x2, matrix products, products(): jnp.dot(pieces[0], col_first, preferred_element_type=jnp.float32)  20 us
    dot_general x2, matrix products, products(): square = jnp.dot(pieces[0], col_zero, preferred_element_type=jnp.float32)  19.5 us
    dot_general x2, matrix products, products(): jnp.dot(pieces[1], col_zero, preferred_element_type=jnp.float32)  19.3 us
    scatter x1, local copies, waits for them, and re-layouts, on_device(): sent_strips = jnp.zeros((devices * capacity, atom_width, block_width), st...  13.3 us
  transfers between devices with their start and end apart: 10, of which 7 were waited for; matrix products, arithmetic and copies ran while one was open for 17% of the time, Pallas kernels for 0%

profile of v1, /device:TPU:0, one launch (start us, length us, event | category | flops | bytes accessed | tf_op | source)
XLA Modules:
  0.0 440.9 jit_solution(8285399760148214577)
XLA Ops:
  7.2 0.7 all-gather.9.cloned.1.call-update
  8.0 0.7 all-gather.7.cloned.1.call-update
  8.9 1.1 scatter_custom_fusion.1
  10.0 0.8 all_to_all.23
  10.8 11.1 %all-to-all-start.1 = ((s32[128,1,2]{2,1,0:T(1,128)}), s32[128,1,2]{2,1,0:T(1,128)S(1)}, u32[]{:S(2)}, u32[]{:S(2)}) async-start(s32[128,1,2]{2,1,0:T(1,128)} %bitcast.10), calls=%async_computation.1 | async-start | bytes 131072 | tf_op jit(solution)/shard_map/all_to_all | solution.py:79
  22.5 1.1 scatter_custom_fusion
  23.6 0.8 all_to_all.21
  24.4 7.0 %all-to-all-done.1 = s32[128,1,2]{2,1,0:T(1,128)S(1)} async-done(((s32[128,1,2]{2,1,0:T(1,128)}), s32[128,1,2]{2,1,0:T(1,128)S(1)}, u32[]{:S(2)}, u32[]{:S(2)}) %all-to-all-start.1) | async-done | bytes 1056 | tf_op jit(solution)/shard_map/all_to_all | solution.py:79
  31.3 4.6 %all-to-all-start = ((s32[128,1,2]{2,1,0:T(1,128)}), s32[128,1,2]{2,1,0:T(1,128)S(1)}, u32[]{:S(2)}, u32[]{:S(2)}) async-start(s32[128,1,2]{2,1,0:T(1,128)} %bitcast.9), calls=%async_computation | async-start | bytes 131072 | tf_op jit(solution)/shard_map/all_to_all | solution.py:72
  36.0 0.9 broadcast_in_dim.50
  36.9 13.3 %scatter_fusion = bf16[256,8,128]{2,1,0:T(8,128)(2,1)} fusion(bf16[256,8,128]{2,1,0:T(8,128)(2,1)} %broadcast_in_dim.50, s32[128]{0:T(128)S(1)} %fusion.18, bf16[128,8,128]{2,1,0:T(8,128)(2,1)S(1)} %copy-done.3), kind=kCustom, calls=%fused_computation.2 | custom fusion | bytes 786944 | tf_op jit(solution)/shard_map/scatter | solution.py:60
  50.7 0.7 reduce.6
  51.6 9.8 %all-to-all-start.2 = ((bf16[128,2,8,128]{3,2,1,0:T(8,128)(2,1)}), bf16[128,2,8,128]{3,2,1,0:T(8,128)(2,1)S(1)}, u32[]{:S(2)}, u32[]{:S(2)}) async-start(bf16[128,2,8,128]{3,2,1,0:T(8,128)(2,1)} %bitcast.13), calls=%async_computation.2 | async-start | bytes 1048576 | tf_op jit(solution)/shard_map/all_to_all | solution.py:65
  61.4 0.7 reduce.7
  62.7 12.3 %all-to-all-done.2 = bf16[128,2,8,128]{3,2,1,0:T(8,128)(2,1)S(1)} async-done(((bf16[128,2,8,128]{3,2,1,0:T(8,128)(2,1)}), bf16[128,2,8,128]{3,2,1,0:T(8,128)(2,1)S(1)}, u32[]{:S(2)}, u32[]{:S(2)}) %all-to-all-start.2) | async-done | bytes 524320 | tf_op jit(solution)/shard_map/all_to_all | solution.py:65
  75.6 0.7 copy.73
  76.7 0.9 fusion.12
  78.3 60.5 %all-gather.7.cloned.1.call-done = bf16[768,6144]{1,0:T(8,128)(2,1)} async-done(((bf16[768,384]{1,0:T(8,128)(2,1)}), bf16[768,6144]{1,0:T(8,128)(2,1)}) %all-gather.7.cloned.1.call-update) | async-done | bytes 9437200 | tf_op jit(solution)/shard_map/all_gather | solution.py:27
  138.8 9.7 %fusion.10 = bf16[768,384]{1,0:T(8,128)(2,1)} fusion(f32[768,384]{1,0:T(8,128)S(1)} %copy.45, bf16[768,6144]{1,0:T(8,128)(2,1)} %all-gather.7.cloned.1.call-done, bf16[6144,384]{1,0:T(8,128)(2,1)} %all-gather.9.cloned.1.call-done), kind=kOutput, calls=%fused_computation.18 | convolution fusion | flops 3624763392 | bytes 15925248 | tf_op jit(solution)/shard_map/dot_general | solution.py:30
  149.9 2.6 stack.4
  152.5 4.6 %all-to-all-start.3 = ((bf16[8,768,384]{2,1,0:T(8,128)(2,1)}), bf16[8,768,384]{2,1,0:T(8,128)(2,1)}, u32[]{:S(2)}, u32[]{:S(2)}) async-start(bf16[8,768,384]{2,1,0:T(8,128)(2,1)} %stack.4), calls=%async_computation.3 | async-start | bytes 9437184 | tf_op jit(solution)/shard_map/all_to_all | solution.py:24
  157.9 58.6 %all-gather.15.cloned.1.call-done = bf16[768,6144]{0,1:T(8,128)(2,1)} async-done(((bf16[768,384]{0,1:T(8,128)(2,1)}), bf16[768,6144]{0,1:T(8,128)(2,1)}) %all-gather.15.cloned.1.call-update) | async-done | bytes 9437200 | tf_op jit(solution)/shard_map/all_gather | solution.py:28
  216.5 9.2 %fusion.24 = f32[768,384]{1,0:T(8,128)S(1)} fusion(bf16[768,6144]{0,1:T(8,128)(2,1)} %all-gather.15.cloned.1.call-done, bf16[6144,384]{1,0:T(8,128)(2,1)} %all-gather.9.cloned.1.call-done), kind=kOutput, calls=%fused_computation.56 | convolution fusion | flops 3623878656 | bytes 15335424 | tf_op jit(solution)/shard_map/dot_general | solution.py:32
  225.7 10.2 %fusion.9 = bf16[768,384]{1,0:T(8,128)(2,1)} fusion(f32[768,384]{1,0:T(8,128)S(1)} %copy.57, f32[768,384]{1,0:T(8,128)S(1)} %fusion.24, bf16[768,6144]{1,0:T(8,128)(2,1)} %all-gather.7.cloned.1.call-done, bf16[6144,384]{1,0:T(8,128)(2,1)} %bitcast.19), kind=kOutput, calls=%fused_computation.17 | convolution fusion | flops 3625058304 | bytes 17104896 | tf_op jit(solution)/shard_map/dot_general | solution.py:31
  235.9 1.5 stack.5
  237.4 60.2 %all_to_all.33 = bf16[8,768,384]{2,1,0:T(8,128)(2,1)} all-to-all(bf16[8,768,384]{2,1,0:T(8,128)(2,1)S(1)} %stack.5), channel_id=1, replica_groups=mesh['row'=8,'col'=16] {'row'}, dimensions={0} | all-to-all | bytes 9437184 | tf_op jit(solution)/shard_map/all_to_all | solution.py:24
  297.6 4.9 %all-gather.11.cloned.1.call-done = bf16[768,6144]{1,0:T(8,128)(2,1)} async-done(((bf16[768,384]{1,0:T(8,128)(2,1)}), bf16[768,6144]{1,0:T(8,128)(2,1)}) %all-gather.11.cloned.1.call-update) | async-done | bytes 9437200 | tf_op jit(solution)/shard_map/all_gather | solution.py:27
  302.5 9.8 %fusion.25 = f32[768,384]{1,0:T(8,128)} fusion(bf16[768,6144]{1,0:T(8,128)(2,1)} %all-gather.11.cloned.1.call-done, bf16[6144,384]{1,0:T(8,128)(2,1)} %bitcast.90), kind=kOutput, calls=%fused_computation.57 | convolution fusion | flops 3623878656 | bytes 15335424 | tf_op jit(solution)/shard_map/dot_general | solution.py:31
  312.3 25.8 %all-gather.13.cloned.1.call-done = bf16[6144,384]{1,0:T(8,128)(2,1)} async-done(((bf16[768,384]{1,0:T(8,128)(2,1)}), bf16[6144,384]{1,0:T(8,128)(2,1)}) %all-gather.13.cloned.1.call-update) | async-done | bytes 4718608 | tf_op jit(solution)/shard_map/all_gather | solution.py:23
  338.1 9.8 %fusion.2 = f32[768,384]{1,0:T(8,128)} fusion(f32[768,384]{1,0:T(8,128)S(1)} %copy.45, bf16[768,6144]{1,0:T(8,128)(2,1)} %all-gather.11.cloned.1.call-done, bf16[6144,384]{1,0:T(8,128)(2,1)} %all-gather.13.cloned.1.call-done, bf16[768,384]{1,0:T(8,128)(2,1)S(1)} %copy-done.1), kind=kOutput, calls=%fused_computation.9 | convolution fusion | flops 3625353216 | bytes 17104896 | tf_op jit(solution)/shard_map/dot_general | solution.py:30
  347.9 76.1 %all-gather.17.cloned.1.call-done = bf16[768,6144]{1,0:T(8,128)(2,1)} async-done(((bf16[768,384]{1,0:T(8,128)(2,1)}), bf16[768,6144]{1,0:T(8,128)(2,1)}) %all-gather.17.cloned.1.call-update) | async-done | bytes 9437200 | tf_op jit(solution)/shard_map/all_gather | solution.py:28
  424.0 10.1 %fusion.8 = f32[768,384]{1,0:T(8,128)} fusion(f32[768,384]{1,0:T(8,128)S(1)} %copy.57, f32[768,384]{1,0:T(8,128)} %fusion.25, bf16[768,6144]{1,0:T(8,128)(2,1)} %all-gather.17.cloned.1.call-done, bf16[6144,384]{1,0:T(8,128)(2,1)} %all-gather.13.cloned.1.call-done, bf16[768,384]{1,0:T(8,128)(2,1)S(1)} %copy-done.2), kind=kOutput, calls=%fused_computation.16 | convolution fusion | flops 3625648128 | bytes 18284544 | tf_op jit(solution)/shard_map/dot_general | solution.py:32
  (59 shorter events, 5.8 us)
Async XLA Ops:
  7.2 1.5 copy-start.5
  7.2 14.7 %copy-start.4 = (s32[3,48,48]{2,1,0:T(8,128)S(1)}, s32[3,48,48]{2,1,0:T(8,128)}, u32[]{:S(2)}) copy-start(s32[3,48,48]{2,1,0:T(8,128)} %param.11) | copy-start | bytes 82948
  7.2 29.7 %copy-start.3 = (bf16[128,8,128]{2,1,0:T(8,128)(2,1)S(1)}, bf16[128,8,128]{2,1,0:T(8,128)(2,1)}, u32[]{:S(2)}) copy-start(bf16[128,8,128]{2,1,0:T(8,128)(2,1)} %param.7) | copy-start | bytes 786436
  7.2 71.1 %all-gather.9.cloned.1.call-start = ((), (), s32[]{:S(2)}) async-start(), calls=%async_computation.6 | async-start | bytes 5308416 | tf_op jit(solution)/shard_map/all_gather | solution.py:23
  7.9 130.9 %all-gather.7.cloned.1.call-start = ((), (), s32[]{:S(2)}) async-start(), calls=%async_computation.5 | async-start | bytes 10027008 | tf_op jit(solution)/shard_map/all_gather | solution.py:27
  10.8 20.6 %all-to-all-start.1 = ((s32[128,1,2]{2,1,0:T(1,128)}), s32[128,1,2]{2,1,0:T(1,128)S(1)}, u32[]{:S(2)}, u32[]{:S(2)}) async-start(s32[128,1,2]{2,1,0:T(1,128)} %bitcast.10), calls=%async_computation.1 | async-start | bytes 131072 | tf_op jit(solution)/shard_map/all_to_all | solution.py:79
  31.3 20.3 %all-to-all-start = ((s32[128,1,2]{2,1,0:T(1,128)}), s32[128,1,2]{2,1,0:T(1,128)S(1)}, u32[]{:S(2)}, u32[]{:S(2)}) async-start(s32[128,1,2]{2,1,0:T(1,128)} %bitcast.9), calls=%async_computation | async-start | bytes 131072 | tf_op jit(solution)/shard_map/all_to_all | solution.py:72
  51.6 23.4 %all-to-all-start.2 = ((bf16[128,2,8,128]{3,2,1,0:T(8,128)(2,1)}), bf16[128,2,8,128]{3,2,1,0:T(8,128)(2,1)S(1)}, u32[]{:S(2)}, u32[]{:S(2)}) async-start(bf16[128,2,8,128]{3,2,1,0:T(8,128)(2,1)} %bitcast.13), calls=%async_computation.2 | async-start | bytes 1048576 | tf_op jit(solution)/shard_map/all_to_all | solution.py:65
  61.4 155.1 %all-gather.15.cloned.1.call-start = ((), (), s32[]{:S(2)}) async-start(), calls=%async_computation.9 | async-start | bytes 10027008 | tf_op jit(solution)/shard_map/all_gather | solution.py:28
  77.7 224.8 %all-gather.11.cloned.1.call-start = ((), (), s32[]{:S(2)}) async-start(), calls=%async_computation.7 | async-start | bytes 10027008 | tf_op jit(solution)/shard_map/all_gather | solution.py:27
  148.5 1.1 copy-start
  148.5 189.6 %all-gather.13.cloned.1.call-start = ((), (), s32[]{:S(2)}) async-start(), calls=%async_computation.8 | async-start | bytes 5308416 | tf_op jit(solution)/shard_map/all_gather | solution.py:23
  152.5 73.2 %all-to-all-start.3 = ((bf16[8,768,384]{2,1,0:T(8,128)(2,1)}), bf16[8,768,384]{2,1,0:T(8,128)(2,1)}, u32[]{:S(2)}, u32[]{:S(2)}) async-start(bf16[8,768,384]{2,1,0:T(8,128)(2,1)} %stack.4), calls=%async_computation.3 | async-start | bytes 9437184 | tf_op jit(solution)/shard_map/all_to_all | solution.py:24
  157.1 266.9 %all-gather.17.cloned.1.call-start = ((), (), s32[]{:S(2)}) async-start(), calls=%async_computation.10 | async-start | bytes 10027008 | tf_op jit(solution)/shard_map/all_gather | solution.py:28
  302.5 35.6 %copy-start.1 = (bf16[768,384]{1,0:T(8,128)(2,1)S(1)}, bf16[768,384]{1,0:T(8,128)(2,1)}, u32[]{:S(2)}) copy-start(bf16[768,384]{1,0:T(8,128)(2,1)} %fusion.10) | copy-start | bytes 1769476
  312.3 111.7 %copy-start.2 = (bf16[768,384]{1,0:T(8,128)(2,1)S(1)}, bf16[768,384]{1,0:T(8,128)(2,1)}, u32[]{:S(2)}) copy-start(bf16[768,384]{1,0:T(8,128)(2,1)} %fusion.9) | copy-start | bytes 1769476
Sparse Core Ops, SparseCore 0:
  9.7 37.4 all-gather.8
  49.3 89.4 all-gather.6
  141.5 74.9 all-gather.14
  219.0 83.4 all-gather.10
  304.6 33.4 all-gather.12
  340.1 83.8 all-gather.16
